TPU v7x, 512 devices: a whole 4x8x8 slice. The times are simulated.
512 devices in a mesh: band: 4 (over x), tm: 128 (over y, z, core).
Axes of the slice: x: 4, y: 8, z: 8, core: 2. Of those that a mesh axis runs over, the one named last changes fastest.
Arguments:
- timeline: bfloat16 [65536, 1024], P('tm', 'band'), parts along dimension 1, may hold values from -6 to 6
- pointing: int32 [65536, 1024], P('tm', 'band'), parts along dimension 1, may hold values from 0 to 127
- plate_angle: float32 [65536], P('tm'), may hold values from -3.140625 to 3.140625
- detector_angle: float32 [1024], P('band'), parts along dimension 0, may hold values from -3.140625 to 3.140625
- detector_weight: float32 [1024], P('band'), parts along dimension 0, may hold values from 0.3 to 3
- kernel: bfloat16 [4100], P('band'), parts along dimension 0, may hold values from -0.1875 to 0.1875
- tile_owner: int32 [8192, 4], P('tm', 'band'), parts along dimension 1, may hold values from 0 to 127; in each aligned block of 64 rows (0 to 63, 64 to 127, ...) at most 2 rows name the same one
- tile_block: int32 [8192, 4], P('tm', 'band'), parts along dimension 1, may hold values from 0 to 511
- wiener: float32 [12, 4096, 2048], P('band', 'tm'), parts along dimension 0, may hold values from 0.05 to 1
Outputs:
- filtered_spectrum: float32 [2, 12, 4096, 2048], P(None, 'band', 'tm'), parts along dimension 1
There are 4 independent parts, one for each index of `band`. A program takes and returns all parts, laid end to end along the dimension named above; an argument that names none is the same for every part. Nothing has to cross between parts.
Inputs may be any that keep to these rules, and one draw needn't show every extreme that they name: `tile_owner`: at most 2 of the 64 tiles of one time shard name the same owner, some shard's tiles name one owner exactly 2 times, and every owner is named by some tile.
All inputs are finite; a program needn't handle non-finite values.
Results may differ from a plain program's by a relative error of at most 0.0029.
Values may be sent and summed in bfloat16 or wider, within the bound.
A program may use at most 128 MiB of HBM per device.

v0:
```python
import functools
import math

import jax
import jax.numpy as jnp
import numpy as np
from jax import lax
from jax.experimental import pallas as pl
from jax.experimental.pallas import tpu as pltpu
from jax.sharding import PartitionSpec as P

DET = 256
TS = 512
PIECE = 16
DGRP = 128
BPIX = 128
ROWS = 2048
COLS = 4096
NTILE = 64
N_TM = 128
SIDE = 8
TAPS_PAD = 1280
MESH = pl.DeviceIdType.MESH
F32 = jnp.float32
BF16 = jnp.bfloat16


def ring_dist(d):
    return min(d, SIDE - d)


def dot(a, b, dims=((1,), (0,))):
    return lax.dot_general(a, b, (dims, ((), ())), preferred_element_type=F32)


def iota(shape, axis):
    return lax.broadcasted_iota(jnp.int32, shape, axis)


def map_kernel(
    timeline, pointing, plate, det_angle, det_weight, taps, owner, block,
    rows_out,
    window, toep, trig, vals, pixels, spread, low_hot, local, gathered, meta, basis, turn,
    halo_send, halo_recv, m1_send, m1_recv, m2_send, m2_recv,
    p1_send, p1_recv, p2_send, p2_recv, sib_send, sib_recv,
):
    band = lax.axis_index("band")
    me = lax.axis_index("tm")
    y = me // 16
    z = (me // 2) % SIDE
    c = me % 2
    zc = me % 16

    def dev(yy, zz, cc):
        return (band, (yy % SIDE) * 16 + (zz % SIDE) * 2 + cc)

    right, left = (band, (me + 1) % N_TM), (band, (me + N_TM - 1) % N_TM)
    plane = [(band, y * 16 + (zc + k) % 16) for k in range(1, 16)]
    column = [dev(y + k, z, c) for k in range(1, SIDE)]
    barrier = pltpu.get_barrier_semaphore()
    for other in plane + column + [right, left]:
        pl.semaphore_signal(barrier, inc=1, device_id=other, device_id_type=MESH)

    lane = iota((NTILE, 128), 1)
    q, a = (lane % NTILE) // 8, lane % 8
    wanted = ((q // 2) * 8 + a) * 2 + q % 2
    place = jnp.where((lane // NTILE == c) & (wanted == iota((NTILE, 128), 0)), 1.0, 0.0)
    sub = iota((8, NTILE), 0)
    parts = jnp.where(
        sub == 0, owner[...], jnp.where(sub == 1, block[...] // 32, block[...] % 32)
    ).astype(F32)
    spots = dot(parts.astype(BF16), place.astype(BF16)).astype(jnp.int32)
    meta[y, zc] = (spots[0:1] * 16 + spots[1:2]) * 32 + spots[2:3]

    pl.semaphore_wait(barrier, 24)

    def remote(src, dst, send, recv, to):
        copy = pltpu.make_async_remote_copy(
            src_ref=src, dst_ref=dst, send_sem=send, recv_sem=recv, device_id=to, device_id_type=MESH
        )
        copy.start()
        return copy

    pending = []
    halo = [
        remote(timeline, window.at[pl.ds(0, TS)], halo_send.at[0], halo_recv.at[0], right),
        remote(timeline, window.at[pl.ds(2 * TS, TS)], halo_send.at[1], halo_recv.at[1], left),
    ]
    first_meta = [
        remote(meta.at[y, zc], meta.at[y, zc], m1_send.at[k], m1_recv.at[k], to)
        for k, to in enumerate(plane)
    ]

    window[TS : 2 * TS, :] = timeline[...]
    band_rows = jnp.broadcast_to(taps[...], (256, TAPS_PAD))
    toep[...] = pltpu.roll(band_rows, 0, 1, stride=1, stride_axis=0).astype(BF16)
    for half in range(2):
        pixels[half] = pointing[:, half * 128 : half * 128 + 128]
    for part in range(4):
        turned = jnp.transpose(jnp.broadcast_to(plate[part : part + 1, :], (128, 128)))
        for half in range(2):
            lanes = slice(half * 128, half * 128 + 128)
            angle = 2.0 * turned + det_angle[:, lanes]
            trig[0, part * 128 : part * 128 + 128, lanes] = jnp.cos(2.0 * angle)
            trig[1, part * 128 : part * 128 + 128, lanes] = jnp.sin(2.0 * angle)
    row = iota((BPIX, 128), 0)
    lane = iota((BPIX, 128), 1)
    pixel = (row % 8) * 16 + row // 8
    step = (((me * 32 + lane % 32) * pixel) % COLS).astype(F32) * (2.0 * math.pi / COLS)
    cos_x, sin_x = jnp.cos(step), jnp.sin(step)
    for s in range(3):
        mine = lane // 32 == s
        whole = jnp.concatenate([jnp.where(mine, cos_x, 0.0), jnp.where(mine, -sin_x, 0.0)], axis=1)
        high = whole.astype(BF16)
        basis[s * 128 : s * 128 + 128, :] = high
        basis[384 + s * 128 : 384 + s * 128 + 128, :] = (whole - high.astype(F32)).astype(BF16)
    step = ((iota((32, 128), 0) * (iota((32, 128), 1) % 32)) % 32).astype(F32) * (2.0 * math.pi / 32)
    whole = jnp.concatenate([jnp.cos(step), jnp.sin(step)], axis=1)
    high = whole.astype(BF16)
    turn[0:32, :] = high
    turn[32:64, :] = (whole - high.astype(F32)).astype(BF16)
    rows_out[...] = jnp.zeros_like(rows_out)

    for copy in first_meta:
        copy.wait_recv()
    second_meta = [
        remote(meta.at[y], meta.at[y], m2_send.at[k], m2_recv.at[k], to)
        for k, to in enumerate(column)
    ]
    for copy in halo:
        copy.wait_recv()

    @pl.when(me == 0)
    def _():
        window[0:TS, :] = jnp.zeros((TS, DET), BF16)

    @pl.when(me == N_TM - 1)
    def _():
        window[2 * TS : 3 * TS, :] = jnp.zeros((TS, DET), BF16)

    for part in range(2):
        rows = slice(part * 256, part * 256 + 256)
        filtered = dot(toep[...], window[part * 256 : part * 256 + TAPS_PAD, :])
        weighted = det_weight[...] * filtered
        for half in range(2):
            lanes = slice(half * 128, half * 128 + 128)
            vals[half, rows, :] = weighted[:, lanes]
            vals[2 + half, rows, :] = weighted[:, lanes] * trig[0, rows, lanes]
            vals[4 + half, rows, :] = weighted[:, lanes] * trig[1, rows, lanes]

    lane = iota((8, 128), 1)
    pick = (lane // 8) * 8 + iota((8, 128), 0)

    def bin_tiles(q, carry):
        first = (q // 2) * 128
        for t in range(PIECE):
            where = pl.ds(first + t, 8, stride=PIECE)
            pixel = pixels[q % 2, where, :]
            high, low = pixel // 16, pixel % 16
            value = [vals[2 * s + q % 2, where, :] for s in range(3)]
            at = slice(t * 128, t * 128 + 128)
            for pair in range(12):
                both = []
                for k in (2 * pair, 2 * pair + 1):
                    both.append(jnp.where(high == k // 3, value[k % 3], 0.0))
                spread[pair * 16 : pair * 16 + 16, at] = jnp.concatenate(both, axis=0).astype(BF16)
            for pair in range(8):
                both = [jnp.where(low == k, 1.0, 0.0) for k in (2 * pair, 2 * pair + 1)]
                low_hot[pair * 16 : pair * 16 + 16, at] = jnp.concatenate(both, axis=0).astype(BF16)
        crossed = dot(spread[...], low_hot[...], ((1,), (1,)))
        for s in range(3):
            total = jnp.zeros((8, 128), F32)
            for h in range(8):
                k = h * 3 + s
                own = jnp.take_along_axis(crossed[k * 8 : k * 8 + 8], pick, axis=1)
                total = jnp.where(lane % 8 == h, own, total)
            local[pl.ds(pl.multiple_of(q * 8, 8), 8), s * 128 : s * 128 + 128] = total
        return carry

    lax.fori_loop(0, 8, bin_tiles, 0)

    for copy in second_meta:
        copy.wait_recv()
    pending += halo + first_meta + second_meta

    c1, c0 = c, 1 - c
    up = dev(y + c0, z + c1, c)
    down = dev(y + SIDE - c0, z + SIDE - c1, c)
    peers = [dev(y + c1 * k, z + c0 * k, c) for k in range(1, SIDE)]
    sibling = dev(y, z, 1 - c)

    def chip(d2, d1):
        return ((y + 16 - c1 * d1 - c0 * d2) % SIDE) * SIDE + (z + 16 - c0 * d1 - c1 * d2) % SIDE

    half = pl.ds(pl.multiple_of(c * NTILE, NTILE), NTILE)
    gathered[y * SIDE + z, half] = local[...].astype(BF16)

    def forward(d2, d1, send, recv, to):
        piece = gathered.at[chip(d2, d1), half]
        return remote(piece, piece, send, recv, to)

    arriving = {}
    siblings = {}
    order = sorted(
        (ring_dist(d2) + ring_dist(d1) / 4, ring_dist(d1), d2, d1)
        for d2 in range(SIDE)
        for d1 in range(SIDE)
    )

    def along_second(d2, d1):
        k = d2 + 1
        if d2 < 3 or (d2 == 3 and d1 < 4):
            arriving[k, d1] = forward(d2, d1, p2_send.at[k * 8 + d1], p2_recv.at[k * 8 + d1], up)
        k = (d2 + 7) % SIDE
        if d2 in (0, 6, 7) or (d2 == 5 and d1 >= 4):
            arriving[k, d1] = forward(d2, d1, p2_send.at[k * 8 + d1], p2_recv.at[k * 8 + d1], down)

    key_rows = iota((256, 512), 0)
    turn_rows = iota((64, 512), 0) % 32

    def use(chips):
        tiles = jnp.concatenate([gathered[i] for i in chips], axis=0)
        codes = jnp.concatenate(
            [meta[i // SIDE, (i % SIDE) * 2] + meta[i // SIDE, (i % SIDE) * 2 + 1] for i in chips],
            axis=1,
        )
        spectra = dot(tiles, basis[0:384]) + dot(tiles, basis[384:768])
        turn_hot = jnp.where(turn_rows == codes % 32, 1.0, 0.0).astype(BF16)
        turned = dot(turn_hot, turn[...], ((0,), (0,)))
        real, imag = spectra[:, 0:128], spectra[:, 128:256]
        cos_b, sin_b = turned[:, 0:128], turned[:, 128:256]
        moved = jnp.concatenate(
            [real * cos_b + imag * sin_b, imag * cos_b - real * sin_b], axis=1
        ).astype(BF16)
        map_row = codes // 32
        low, high = map_row % 8, map_row // 8

        def add(r, carry):
            key = jnp.where(low == r, high, -1)
            hot = jnp.where(key_rows == key, 1.0, 0.0).astype(BF16)
            at = pl.ds(pl.multiple_of(r * 256, 256), 256)
            rows_out[at, :] += dot(hot, moved)
            return carry

        lax.fori_loop(0, 8, add, 0)

    turn_at = {(e[2], e[3]): n for n, e in enumerate(order)}
    ready = sorted((max(turn_at[i, j], turn_at[j, i]), i, j) for i, j in turn_at)
    used = 0

    def use_ready(reached):
        nonlocal used
        while used < len(ready) and ready[used + 3][0] <= reached:
            group = [(i, j) for _, i, j in ready[used : used + 4]]
            used += 4
            for i, j in group:
                siblings[j, i].wait_recv()
            use([chip(i, j) for i, j in group])

    lag = 6
    for n, (_, _, d2, d1) in enumerate(order):
        if n:
            arriving[d2, d1].wait_recv()
        along_second(d2, d1)
        if n == 0:
            for k in (1, 7, 2, 6, 3, 5, 4):
                arriving[0, k] = forward(0, 0, p1_send.at[k], p1_recv.at[k], peers[k - 1])
        siblings[d2, d1] = forward(
            d2, d1, sib_send.at[d2 * 8 + d1], sib_recv.at[d2 * 8 + d1], sibling
        )
        use_ready(n - lag)
    use_ready(len(order))
    pending += list(arriving.values()) + list(siblings.values())
    for copy in pending:
        copy.wait_send()


def eighth(parts):
    def add(u, v):
        return (u[0] + v[0], u[1] + v[1])

    def sub(u, v):
        return (u[0] - v[0], u[1] - v[1])

    def turn(u):
        return (u[1], -u[0])

    def four(u):
        s, d, t, e = add(u[0], u[2]), sub(u[0], u[2]), add(u[1], u[3]), turn(sub(u[1], u[3]))
        return [add(s, t), add(d, e), sub(s, t), sub(d, e)]

    even, odd = four(parts[0::2]), four(parts[1::2])
    h = math.sqrt(0.5)
    odd[1] = ((odd[1][0] + odd[1][1]) * h, (odd[1][1] - odd[1][0]) * h)
    odd[2] = turn(odd[2])
    odd[3] = ((odd[3][1] - odd[3][0]) * h, (-odd[3][0] - odd[3][1]) * h)
    return [add(even[k], odd[k]) for k in range(4)] + [sub(even[k], odd[k]) for k in range(4)]


def column_kernel(rows, high, low, wiener, out):
    lines = []
    for r in range(8):
        at = slice(r * 256, r * 256 + 256)
        both = jnp.concatenate(
            [jnp.transpose(rows[at, 0:128])[0:96], jnp.transpose(rows[at, 128:256])[0:96]], axis=0
        )
        upper = both.astype(BF16)
        stacked = jnp.concatenate([upper, (both - upper.astype(F32)).astype(BF16)], axis=0)
        waves = []
        for w in range(2):
            wide = dot(stacked, high[r, w])
            waves.append(wide[0:192] + wide[192:384] + dot(upper, low[r, w]))
        lines.append((waves[0][0:96] + waves[1][96:192], waves[0][96:192] - waves[1][0:96]))
    scale = 1.0 / math.sqrt(ROWS * COLS)
    for k, (real, imag) in enumerate(eighth(lines)):
        at = slice(k * 256, k * 256 + 256)
        for s in range(3):
            gain = wiener[s, :, at] * scale
            out[0, s, :, at] = real[s * 32 : s * 32 + 32] * gain
            out[1, s, :, at] = imag[s * 32 : s * 32 + 32] * gain


def column_tables():
    r0 = np.arange(256)[None, :, None]
    r1 = np.arange(8)[:, None, None]
    k = np.arange(256)[None, None, :]
    phase = (k * (r1 + 8 * r0) % ROWS) * (2.0 * np.pi / ROWS)
    table = np.stack([np.cos(phase), np.sin(phase)], axis=1)
    high = table.astype(BF16)
    low = (table - high.astype(np.float64)).astype(BF16)
    return high, low


def owned_rows(timeline, pointing, plate_angle, detector_angle, detector_weight, kernel, tile_owner, tile_block):
    taps = jnp.pad(kernel.astype(F32), (0, TAPS_PAD - kernel.shape[0])).reshape(1, TAPS_PAD)
    vmem = pl.BlockSpec(memory_space=pltpu.VMEM)
    dma = pltpu.SemaphoreType.DMA
    return pl.pallas_call(
        map_kernel,
        out_shape=jax.ShapeDtypeStruct((ROWS, 256), F32),
        in_specs=[vmem] * 8,
        out_specs=vmem,
        scratch_shapes=[
            pltpu.VMEM((3 * TS, DET), BF16),
            pltpu.VMEM((256, TAPS_PAD), BF16),
            pltpu.VMEM((2, TS, DET), F32),
            pltpu.VMEM((6, TS, 128), F32),
            pltpu.VMEM((2, TS, 128), jnp.int32),
            pltpu.VMEM((192, PIECE * DGRP), BF16),
            pltpu.VMEM((128, PIECE * DGRP), BF16),
            pltpu.VMEM((NTILE, 384), F32),
            pltpu.VMEM((64, 2 * NTILE, 384), BF16),
            pltpu.VMEM((8, 16, 1, 128), jnp.int32),
            pltpu.VMEM((768, 256), BF16),
            pltpu.VMEM((64, 256), BF16),
            dma((2,)), dma((2,)), dma((15,)), dma((15,)), dma((7,)), dma((7,)),
            dma((8,)), dma((8,)), dma((64,)), dma((64,)), dma((64,)), dma((64,)),
        ],
        compiler_params=pltpu.CompilerParams(
            collective_id=0, has_side_effects=True, vmem_limit_bytes=48 << 20
        ),
        cost_estimate=pl.CostEstimate(flops=20 << 30, bytes_accessed=4 << 20, transcendentals=1 << 20),
    )(
        timeline,
        pointing,
        plate_angle.reshape(4, 128),
        detector_angle.reshape(1, DET),
        detector_weight.reshape(1, DET),
        taps,
        tile_owner.reshape(1, NTILE),
        tile_block.reshape(1, NTILE),
    )


def columns(rows, wiener):
    vmem = pl.BlockSpec(memory_space=pltpu.VMEM)
    high, low = column_tables()
    return pl.pallas_call(
        column_kernel,
        out_shape=jax.ShapeDtypeStruct((2, 3, 32, ROWS), F32),
        in_specs=[vmem] * 4,
        out_specs=vmem,
        compiler_params=pltpu.CompilerParams(vmem_limit_bytes=48 << 20),
        cost_estimate=pl.CostEstimate(flops=4 << 30, bytes_accessed=9 << 20, transcendentals=0),
    )(rows, jnp.asarray(high), jnp.asarray(low), wiener)


def body(*arrays):
    return columns(owned_rows(*arrays[:8]), arrays[8])


def solution(mesh):
    placed = (
        P("tm", "band"),
        P("tm", "band"),
        P("tm"),
        P("band"),
        P("band"),
        P("band"),
        P("tm", "band"),
        P("tm", "band"),
        P("band", "tm", None),
    )
    return jax.shard_map(
        body, mesh=mesh, in_specs=placed, out_specs=P(None, "band", "tm", None), check_vma=False
    )
```

profile of v0, /device:TPU:1, one launch (start us, length us, event | category | flops | bytes accessed | tf_op | source)
XLA Modules:
  0.0 92.6 jit_solution(8363069531234862375)
XLA Ops:
  0.0 0.7 pad_convert_fusion
  0.7 0.0 copy-start.1
  0.7 1.0 %copy-done.1 = s32[512,256]{1,0:T(8,128)S(1)} copy-done((s32[512,256]{1,0:T(8,128)S(1)}, s32[512,256]{1,0:T(8,128)}, u32[]{:S(2)}) %copy-start.1) | copy-done | bytes 524312
  1.7 0.0 copy-start.2
  1.7 0.9 %copy-done.2 = bf16[512,256]{1,0:T(8,128)(2,1)S(1)} copy-done((bf16[512,256]{1,0:T(8,128)(2,1)S(1)}, bf16[512,256]{1,0:T(8,128)(2,1)}, u32[]{:S(2)}) %copy-start.2) | copy-done | bytes 262168
  2.7 0.0 copy-start.3
  2.7 0.7 copy-done.3
  3.4 0.0 copy-start.4
  3.4 0.7 copy-done.4
  4.1 0.0 copy-start.5
  4.1 0.7 copy-done.5
  4.7 0.0 copy-start.6
  4.7 0.7 copy-done.6
  5.4 0.0 copy-start.7
  5.4 0.7 copy-done.7
  6.0 0.0 copy-start
  6.0 0.0 copy-start.8
  6.0 82.0 %shard_map.109.rows = f32[2048,256]{1,0:T(8,128)S(1)} custom-call(bf16[512,256]{1,0:T(8,128)(2,1)S(1)} %copy-done.2, s32[512,256]{1,0:T(8,128)S(1)} %copy-done.1, f32[4,128]{1,0:T(4,128)S(1)} %bitcast.5, f32[1,256]{1,0:T(1,128)S(1)} %bitcast.6, f32[1,256]{1,0:T(1,128)S(1)} %bitcast.7, f32[1,1280]{1,0:T(1,128)S(1)} %reshape.28.taps, s32[1,64]{1,0:T(1,128)S(1)} %bitcast.8, ...), custom_call_target="tpu_custom_call" | custom-call | flops 21474836480 | bytes 4194304 | tf_op jit(solution)/shard_map/pallas_call | solution.py:338
  88.1 0.0 copy-done
  88.1 0.0 copy-done.8
  88.1 4.5 %shard_map.110 = f32[2,3,32,2048]{3,2,1,0:T(8,128)} custom-call(f32[2048,256]{1,0:T(8,128)S(1)} %shard_map.109.rows, bf16[8,2,256,256]{3,2,1,0:T(8,128)(2,1)S(1)} %copy-done.8, bf16[8,2,256,256]{3,2,1,0:T(8,128)(2,1)} %constant.9.clone.low, f32[3,32,2048]{2,1,0:T(8,128)S(1)} %copy-done), custom_call_target="tpu_custom_call" | custom-call | flops 4294967296 | bytes 9437184 | tf_op jit(solution)/shard_map/pallas_call | solution.py:378
  (1 shorter events, 0.0 us)
Async XLA Ops:
  0.7 1.0 %copy-start.1 = (s32[512,256]{1,0:T(8,128)S(1)}, s32[512,256]{1,0:T(8,128)}, u32[]{:S(2)}) copy-start(s32[512,256]{1,0:T(8,128)} %pointing.1) | copy-start | bytes 1572868
  1.7 0.9 %copy-start.2 = (bf16[512,256]{1,0:T(8,128)(2,1)S(1)}, bf16[512,256]{1,0:T(8,128)(2,1)}, u32[]{:S(2)}) copy-start(bf16[512,256]{1,0:T(8,128)(2,1)} %timeline.1) | copy-start | bytes 786436
  2.7 0.7 copy-start.3
  3.4 0.7 copy-start.4
  4.1 0.7 copy-start.5
  4.7 0.7 copy-start.6
  5.4 0.7 copy-start.7
  6.0 82.1 %copy-start = (f32[3,32,2048]{2,1,0:T(8,128)S(1)}, f32[3,32,2048]{2,1,0:T(8,128)}, u32[]{:S(2)}) copy-start(f32[3,32,2048]{2,1,0:T(8,128)} %wiener.1) | copy-start | bytes 2359300
  6.0 82.1 %copy-start.8 = (bf16[8,2,256,256]{3,2,1,0:T(8,128)(2,1)S(1)}, bf16[8,2,256,256]{3,2,1,0:T(8,128)(2,1)}, u32[]{:S(2)}) copy-start(bf16[8,2,256,256]{3,2,1,0:T(8,128)(2,1)} %constant.8.clone.high) | copy-start | bytes 6291460
where the time goes:
time: 92.9 us; the launch traced here: 92.6 us
  Pallas kernels  86.5 us (93%)
  local copies, waits for them, and re-layouts  5.35 us (6%)
    pallas_call x1, Pallas kernels, owned_rows(): pl.pallas_call(map_kernel, out_shape=jax.ShapeDtypeStruct((ROWS, 256), F3...  82 us
    unnamed x18, local copies, waits for them, and re-layouts  5.34 us
    pallas_call x1, Pallas kernels, columns(): pl.pallas_call(column_kernel, out_shape=jax.ShapeDtypeStruct((2, 3, 32, R...  4.5 us

commit v1 on v0

v1 whole, which is shorter than its diff:
```python
import functools
import math

import jax
import jax.numpy as jnp
import numpy as np
from jax import lax
from jax.experimental import pallas as pl
from jax.experimental.pallas import tpu as pltpu
from jax.sharding import PartitionSpec as P

DET = 256
TS = 512
PIECE = 16
DGRP = 128
BPIX = 128
ROWS = 2048
COLS = 4096
NTILE = 64
N_TM = 128
SIDE = 8
TAPS_PAD = 1280
MESH = pl.DeviceIdType.MESH
F32 = jnp.float32
BF16 = jnp.bfloat16


def dot(a, b, dims=((1,), (0,))):
    return lax.dot_general(a, b, (dims, ((), ())), preferred_element_type=F32)


def iota(shape, axis):
    return lax.broadcasted_iota(jnp.int32, shape, axis)


def eighth(parts):
    def add(u, v):
        return (u[0] + v[0], u[1] + v[1])

    def sub(u, v):
        return (u[0] - v[0], u[1] - v[1])

    def turn(u):
        return (u[1], -u[0])

    def four(u):
        s, d, t, e = add(u[0], u[2]), sub(u[0], u[2]), add(u[1], u[3]), turn(sub(u[1], u[3]))
        return [add(s, t), add(d, e), sub(s, t), sub(d, e)]

    even, odd = four(parts[0::2]), four(parts[1::2])
    h = math.sqrt(0.5)
    odd[1] = ((odd[1][0] + odd[1][1]) * h, (odd[1][1] - odd[1][0]) * h)
    odd[2] = turn(odd[2])
    odd[3] = ((odd[3][1] - odd[3][0]) * h, (-odd[3][0] - odd[3][1]) * h)
    return [add(even[k], odd[k]) for k in range(4)] + [sub(even[k], odd[k]) for k in range(4)]


def finish_columns(rows, tables, wiener, out):
    lines = []
    for r in range(8):
        at = slice(r * 256, r * 256 + 256)
        both = jnp.concatenate(
            [jnp.transpose(rows[at, 0:128])[0:96], jnp.transpose(rows[at, 128:256])[0:96]], axis=0
        )
        upper = both.astype(BF16)
        stacked = jnp.concatenate([upper, (both - upper.astype(F32)).astype(BF16)], axis=0)
        waves = []
        for w in range(2):
            wide = dot(stacked, tables[0, r, w])
            waves.append(wide[0:192] + wide[192:384] + dot(upper, tables[1, r, w]))
        lines.append((waves[0][0:96] + waves[1][96:192], waves[0][96:192] - waves[1][0:96]))
    scale = 1.0 / math.sqrt(ROWS * COLS)
    for k, (real, imag) in enumerate(eighth(lines)):
        at = slice(k * 256, k * 256 + 256)
        for s in range(3):
            gain = wiener[s, :, at] * scale
            out[0, s, :, at] = real[s * 32 : s * 32 + 32] * gain
            out[1, s, :, at] = imag[s * 32 : s * 32 + 32] * gain


def map_kernel(
    timeline_in, pointing_in, plate_in, det_angle_in, det_weight_in, taps_in, owner_in, block_in,
    wiener_in, tables_in, out,
    rows, wiener, tables,
    plate, det_angle, det_weight, taps, owner, block, fetched,
    window, toep, trig, vals, pixels, spread, low_hot, local, gathered, meta, basis, turn,
    halo_send, halo_recv, m1_send, m1_recv, m2_send, m2_recv,
    p1_send, p1_recv, p2_send, p2_recv, sib_send, sib_recv,
):
    band = lax.axis_index("band")
    me = lax.axis_index("tm")
    y = me // 16
    z = (me // 2) % SIDE
    c = me % 2
    zc = me % 16

    def dev(yy, zz, cc):
        return (band, (yy % SIDE) * 16 + (zz % SIDE) * 2 + cc)

    def fetch(k, src, dst):
        copy = pltpu.make_async_copy(src, dst, fetched.at[k])
        copy.start()
        return copy

    own = window.at[pl.ds(TS, TS)]
    fetch_codes = [fetch(0, owner_in, owner), fetch(1, block_in, block)]
    fetch_samples = fetch(2, timeline_in, own)
    fetch_rest = [
        fetch(3, plate_in, plate),
        fetch(4, det_angle_in, det_angle),
        fetch(5, det_weight_in, det_weight),
        fetch(6, taps_in, taps),
    ]
    fetch_pixels = [
        fetch(7 + half, pointing_in.at[:, pl.ds(half * 128, 128)], pixels.at[half]) for half in range(2)
    ]

    right, left = (band, (me + 1) % N_TM), (band, (me + N_TM - 1) % N_TM)
    plane = [(band, y * 16 + (zc + k) % 16) for k in range(1, 16)]
    column = [dev(y + k, z, c) for k in range(1, SIDE)]
    barrier = pltpu.get_barrier_semaphore()
    for other in plane + column + [right, left]:
        pl.semaphore_signal(barrier, inc=1, device_id=other, device_id_type=MESH)

    for copy in fetch_codes:
        copy.wait()
    lane = iota((NTILE, 128), 1)
    q, a = (lane % NTILE) // 8, lane % 8
    wanted = ((q // 2) * 8 + a) * 2 + q % 2
    place = jnp.where((lane // NTILE == c) & (wanted == iota((NTILE, 128), 0)), 1.0, 0.0)
    sub = iota((8, NTILE), 0)
    parts = jnp.where(
        sub == 0, owner[...], jnp.where(sub == 1, block[...] // 32, block[...] % 32)
    ).astype(F32)
    spots = dot(parts.astype(BF16), place.astype(BF16)).astype(jnp.int32)
    meta[y, zc] = (spots[0:1] * 16 + spots[1:2]) * 32 + spots[2:3]

    fetch_samples.wait()
    pl.semaphore_wait(barrier, 24)

    def remote(src, dst, send, recv, to):
        copy = pltpu.make_async_remote_copy(
            src_ref=src, dst_ref=dst, send_sem=send, recv_sem=recv, device_id=to, device_id_type=MESH
        )
        copy.start()
        return copy

    pending = []
    halo = [
        remote(own, window.at[pl.ds(0, TS)], halo_send.at[0], halo_recv.at[0], right),
        remote(own, window.at[pl.ds(2 * TS, TS)], halo_send.at[1], halo_recv.at[1], left),
    ]
    first_meta = [
        remote(meta.at[y, zc], meta.at[y, zc], m1_send.at[k], m1_recv.at[k], to)
        for k, to in enumerate(plane)
    ]

    fetch_late = [fetch(9, wiener_in, wiener), fetch(10, tables_in, tables)]
    for copy in fetch_rest:
        copy.wait()
    band_rows = jnp.broadcast_to(taps[...], (256, TAPS_PAD))
    toep[...] = pltpu.roll(band_rows, 0, 1, stride=1, stride_axis=0).astype(BF16)
    plate_cos, plate_sin = jnp.cos(4.0 * plate[...]), jnp.sin(4.0 * plate[...])
    det_cos, det_sin = jnp.cos(2.0 * det_angle[...]), jnp.sin(2.0 * det_angle[...])
    for part in range(4):
        times = slice(part * 128, part * 128 + 128)
        cos_t = jnp.transpose(jnp.broadcast_to(plate_cos[part : part + 1], (128, 128)))
        sin_t = jnp.transpose(jnp.broadcast_to(plate_sin[part : part + 1], (128, 128)))
        for half in range(2):
            lanes = slice(half * 128, half * 128 + 128)
            trig[0, times, lanes] = cos_t * det_cos[:, lanes] - sin_t * det_sin[:, lanes]
            trig[1, times, lanes] = sin_t * det_cos[:, lanes] + cos_t * det_sin[:, lanes]

    rows[...] = jnp.zeros_like(rows)
    for copy in first_meta:
        copy.wait_recv()
    second_meta = [
        remote(meta.at[y], meta.at[y], m2_send.at[k], m2_recv.at[k], to)
        for k, to in enumerate(column)
    ]
    for copy in halo:
        copy.wait_recv()

    @pl.when(me == 0)
    def _():
        window[0:TS, :] = jnp.zeros((TS, DET), BF16)

    @pl.when(me == N_TM - 1)
    def _():
        window[2 * TS : 3 * TS, :] = jnp.zeros((TS, DET), BF16)

    for part in range(2):
        times = slice(part * 256, part * 256 + 256)
        filtered = dot(toep[...], window[part * 256 : part * 256 + TAPS_PAD, :])
        weighted = det_weight[...] * filtered
        for half in range(2):
            lanes = slice(half * 128, half * 128 + 128)
            vals[half, times, :] = weighted[:, lanes]
            vals[2 + half, times, :] = weighted[:, lanes] * trig[0, times, lanes]
            vals[4 + half, times, :] = weighted[:, lanes] * trig[1, times, lanes]

    for copy in fetch_pixels:
        copy.wait()
    lane = iota((8, 128), 1)
    pick = (lane // 8) * 8 + iota((8, 128), 0)

    def bin_tiles(q, carry):
        first = (q // 2) * 128
        for t in range(PIECE):
            where = pl.ds(first + t, 8, stride=PIECE)
            pixel = pixels[q % 2, where, :]
            high, low = pixel // 16, pixel % 16
            value = [vals[2 * s + q % 2, where, :] for s in range(3)]
            at = slice(t * 128, t * 128 + 128)
            for pair in range(12):
                both = []
                for k in (2 * pair, 2 * pair + 1):
                    both.append(jnp.where(high == k // 3, value[k % 3], 0.0))
                spread[pair * 16 : pair * 16 + 16, at] = jnp.concatenate(both, axis=0).astype(BF16)
            for pair in range(8):
                both = [jnp.where(low == k, 1.0, 0.0) for k in (2 * pair, 2 * pair + 1)]
                low_hot[pair * 16 : pair * 16 + 16, at] = jnp.concatenate(both, axis=0).astype(BF16)
        crossed = dot(spread[...], low_hot[...], ((1,), (1,)))
        for s in range(3):
            total = jnp.zeros((8, 128), F32)
            for h in range(8):
                k = h * 3 + s
                own = jnp.take_along_axis(crossed[k * 8 : k * 8 + 8], pick, axis=1)
                total = jnp.where(lane % 8 == h, own, total)
            local[pl.ds(pl.multiple_of(q * 8, 8), 8), s * 128 : s * 128 + 128] = total
        return carry

    lax.fori_loop(0, 8, bin_tiles, 0)

    for copy in second_meta:
        copy.wait_recv()
    pending += halo + first_meta + second_meta

    c1, c0 = c, 1 - c
    up = dev(y + c0, z + c1, c)
    down = dev(y + SIDE - c0, z + SIDE - c1, c)
    peers = [dev(y + c1 * k, z + c0 * k, c) for k in range(1, SIDE)]
    sibling = dev(y, z, 1 - c)

    def chip(d2, d1):
        return ((y + 16 - c1 * d1 - c0 * d2) % SIDE) * SIDE + (z + 16 - c0 * d1 - c1 * d2) % SIDE

    def sibling_chip(d2, d1):
        return ((y + 16 - c0 * d1 - c1 * d2) % SIDE) * SIDE + (z + 16 - c1 * d1 - c0 * d2) % SIDE

    half = pl.ds(pl.multiple_of(c * NTILE, NTILE), NTILE)
    gathered[y * SIDE + z, half] = local[...].astype(BF16)

    def carry(d2, d1, send, recv, to):
        piece = gathered.at[chip(d2, d1), half]
        return pltpu.make_async_remote_copy(
            src_ref=piece, dst_ref=piece, send_sem=send, recv_sem=recv, device_id=to, device_id_type=MESH
        )

    def to_peer(k):
        return carry(0, 0, p1_send.at[k], p1_recv.at[k], peers[k - 1])

    def to_line(d2, d1, step):
        to = up if step == 1 else down
        at = ((d2 + step) % SIDE) * SIDE + d1
        return carry(d2, d1, p2_send.at[at], p2_recv.at[at], to)

    def to_sibling(d2, d1):
        at = d2 * SIDE + d1
        return carry(d2, d1, sib_send.at[at], sib_recv.at[at], sibling)

    to_line(0, 0, 1).start()
    to_line(0, 0, 7).start()
    for k in (1, 2, 3, 7, 6, 5, 4):
        to_peer(k).start()
    to_sibling(0, 0).start()

    row = iota((BPIX, 128), 0)
    lane = iota((BPIX, 128), 1)
    pixel = (row % 8) * 16 + row // 8
    step = (((me * 32 + lane % 32) * pixel) % COLS).astype(F32) * (2.0 * math.pi / COLS)
    cos_x, sin_x = jnp.cos(step), jnp.sin(step)
    for s in range(3):
        mine = lane // 32 == s
        whole = jnp.concatenate([jnp.where(mine, cos_x, 0.0), jnp.where(mine, -sin_x, 0.0)], axis=1)
        high = whole.astype(BF16)
        basis[s * 128 : s * 128 + 128, :] = high
        basis[384 + s * 128 : 384 + s * 128 + 128, :] = (whole - high.astype(F32)).astype(BF16)
    step = ((iota((32, 128), 0) * (iota((32, 128), 1) % 32)) % 32).astype(F32) * (2.0 * math.pi / 32)
    whole = jnp.concatenate([jnp.cos(step), jnp.sin(step)], axis=1)
    high = whole.astype(BF16)
    turn[0:32, :] = high
    turn[32:64, :] = (whole - high.astype(F32)).astype(BF16)

    for d1 in (1, 2, 3, 7, 6, 5, 4):
        to_peer(d1).wait_recv()
        to_line(0, d1, 1).start()
        to_line(0, d1, 7).start()
        to_sibling(0, d1).start()

    def arrive(d2, d1, step):
        to_line((d2 + SIDE - step) % SIDE, d1, step).wait_recv()

    def members(g):
        k = (g + 1) // 2
        single = (7 - g % 7) // 7
        for e in range(8):
            sign, i = e // 4, e % 4
            d2 = (k + sign * (8 - 2 * k)) % SIDE
            d1 = (single * sign + (1 - single) * ((g + 1) % 2)) * 4 + i
            yield d2, d1

    key_rows = iota((256, 1024), 0).astype(F32).astype(BF16)
    turn_rows = iota((64, 1024), 0) % 32

    def each_group(g, state):
        k = 1 + g // 2

        @pl.when(g < 6)
        def _():
            for i in range(4):
                d1 = (g % 2) * 4 + i
                for step in (1, 7):
                    d2 = k if step == 1 else SIDE - k
                    arrive(d2, d1, step)

                    @pl.when(k < 3)
                    def _():
                        to_line(d2, d1, step).start()

                    @pl.when((k == 3) & (g % 2 == (0 if step == 1 else 1)))
                    def _():
                        to_line(d2, d1, step).start()

                    to_sibling(d2, d1).start()

        @pl.when(g == 6)
        def _():
            for d1 in (0, 4, 1, 5, 2, 6, 3, 7):
                arrive(4, d1, 1 if d1 < 4 else 7)
                to_sibling(4, d1).start()

        tiles, codes = [], []
        for d2, d1 in members(g):
            to_sibling(d2, d1).wait_recv()
            mine, other = chip(d2, d1), sibling_chip(d2, d1)
            first, second = mine * c0 + other * c1, mine * c1 + other * c0
            tiles += [gathered[first, 0:NTILE], gathered[second, NTILE : 2 * NTILE]]
            codes.append(
                meta[first // SIDE, (first % SIDE) * 2] + meta[second // SIDE, (second % SIDE) * 2 + 1]
            )
        tiles, codes = jnp.concatenate(tiles, axis=0), jnp.concatenate(codes, axis=1)
        spectra = dot(tiles, basis[0:384]) + dot(tiles, basis[384:768])
        turn_hot = jnp.where(turn_rows == codes % 32, 1.0, 0.0).astype(BF16)
        turned = dot(turn_hot, turn[...], ((0,), (0,)))
        real, imag = spectra[:, 0:128], spectra[:, 128:256]
        cos_b, sin_b = turned[:, 0:128], turned[:, 128:256]
        moved = jnp.concatenate(
            [real * cos_b + imag * sin_b, imag * cos_b - real * sin_b], axis=1
        ).astype(BF16)
        map_row = codes // 32
        low, high = map_row % 8, map_row // 8
        for r in range(8):
            key = jnp.where(low == r, high, -1).astype(F32).astype(BF16)
            hot = jnp.where(key_rows == key, jnp.bfloat16(1), jnp.bfloat16(0))
            rows[r * 256 : r * 256 + 256, :] += dot(hot, moved)
        return state

    lax.fori_loop(0, 8, each_group, 0)

    for copy in fetch_late:
        copy.wait()
    finish_columns(rows, tables, wiener, out)

    for copy in pending:
        copy.wait_send()
    for k in range(1, 8):
        to_peer(k).wait_send()

    def sent(n, state):
        d2, d1 = n // SIDE, n % SIDE
        to_sibling(d2, d1).wait_send()

        @pl.when(d2 > 0)
        def _():
            to_line((d2 + SIDE - 1) % SIDE, d1, 1).wait_send()

        return state

    lax.fori_loop(0, 64, sent, 0)


def column_tables():
    r0 = np.arange(256)[None, :, None]
    r1 = np.arange(8)[:, None, None]
    k = np.arange(256)[None, None, :]
    phase = (k * (r1 + 8 * r0) % ROWS) * (2.0 * np.pi / ROWS)
    table = np.stack([np.cos(phase), np.sin(phase)], axis=1)
    high = table.astype(BF16)
    low = (table - high.astype(np.float64)).astype(BF16)
    return np.stack([high, low])


def body(timeline, pointing, plate_angle, detector_angle, detector_weight, kernel, tile_owner, tile_block, wiener):
    taps = jnp.pad(kernel.astype(F32), (0, TAPS_PAD - kernel.shape[0])).reshape(1, TAPS_PAD)
    vmem = pl.BlockSpec(memory_space=pltpu.VMEM)
    dma = pltpu.SemaphoreType.DMA
    return pl.pallas_call(
        map_kernel,
        out_shape=jax.ShapeDtypeStruct((2, 3, 32, ROWS), F32),
        in_specs=[pl.BlockSpec(memory_space=pl.ANY)] * 10,
        out_specs=vmem,
        scratch_shapes=[
            pltpu.VMEM((ROWS, 256), F32),
            pltpu.VMEM((3, 32, ROWS), F32),
            pltpu.VMEM((2, 8, 2, 256, 256), BF16),
            pltpu.VMEM((4, 128), F32),
            pltpu.VMEM((1, DET), F32),
            pltpu.VMEM((1, DET), F32),
            pltpu.VMEM((1, TAPS_PAD), F32),
            pltpu.VMEM((1, NTILE), jnp.int32),
            pltpu.VMEM((1, NTILE), jnp.int32),
            dma((11,)),
            pltpu.VMEM((3 * TS, DET), BF16),
            pltpu.VMEM((256, TAPS_PAD), BF16),
            pltpu.VMEM((2, TS, DET), F32),
            pltpu.VMEM((6, TS, 128), F32),
            pltpu.VMEM((2, TS, 128), jnp.int32),
            pltpu.VMEM((192, PIECE * DGRP), BF16),
            pltpu.VMEM((128, PIECE * DGRP), BF16),
            pltpu.VMEM((NTILE, 384), F32),
            pltpu.VMEM((64, 2 * NTILE, 384), BF16),
            pltpu.VMEM((8, 16, 1, 128), jnp.int32),
            pltpu.VMEM((768, 256), BF16),
            pltpu.VMEM((64, 256), BF16),
            dma((2,)), dma((2,)), dma((15,)), dma((15,)), dma((7,)), dma((7,)),
            dma((8,)), dma((8,)), dma((64,)), dma((64,)), dma((64,)), dma((64,)),
        ],
        compiler_params=pltpu.CompilerParams(
            collective_id=0, has_side_effects=True, vmem_limit_bytes=64 << 20
        ),
        cost_estimate=pl.CostEstimate(flops=20 << 30, bytes_accessed=4 << 20, transcendentals=1 << 20),
    )(
        timeline,
        pointing,
        plate_angle.reshape(4, 128),
        detector_angle.reshape(1, DET),
        detector_weight.reshape(1, DET),
        taps,
        tile_owner.reshape(1, NTILE),
        tile_block.reshape(1, NTILE),
        wiener,
        jnp.asarray(column_tables()),
    )


def solution(mesh):
    placed = (
        P("tm", "band"),
        P("tm", "band"),
        P("tm"),
        P("band"),
        P("band"),
        P("band"),
        P("tm", "band"),
        P("tm", "band"),
        P("band", "tm", None),
    )
    return jax.shard_map(
        body, mesh=mesh, in_specs=placed, out_specs=P(None, "band", "tm", None), check_vma=False
    )
```

time: 92.9 us -> 78.7 us (0.85)
  Pallas kernels: 86.5 us -> 73.8 us
  local copies, waits for them, and re-layouts: 5.35 us -> 3.3 us
    pallas_call x2 -> x1, Pallas kernels: 86.5 us -> 73.8 us  [body(): pl.pallas_call(map_kernel, out_shape=jax.ShapeDtypeStruct((2, 3, 32, ROWS...]
    unnamed x18 -> x1, local copies, waits for them, and re-layouts: 5.34 us -> 2.7 us
where the time goes in v1:
time: 78.7 us; the launch traced here: 77.8 us
  Pallas kernels  73.8 us (94%)
  local copies, waits for them, and re-layouts  3.3 us (4%)
    pallas_call x1, Pallas kernels, body(): pl.pallas_call(map_kernel, out_shape=jax.ShapeDtypeStruct((2, 3, 32, ROWS...  73.8 us
    unnamed x1, local copies, waits for them, and re-layouts  2.7 us

profile of v1, /device:TPU:1, one launch (start us, length us, event | category | flops | bytes accessed | tf_op | source)
XLA Modules:
  0.0 77.8 jit_solution(12262633402417591751)
XLA Ops:
  0.0 0.7 pad_convert_fusion
  0.7 0.6 reshape.28.taps_in
  1.3 73.8 %shard_map.100 = f32[2,3,32,2048]{3,2,1,0:T(8,128)} custom-call(bf16[512,256]{1,0:T(8,128)(2,1)} %timeline_in.1, s32[512,256]{1,0:T(8,128)} %pointing_in.1, f32[4,128]{1,0:T(4,128)} %bitcast.5, f32[1,256]{1,0:T(1,128)} %bitcast.6, f32[1,256]{1,0:T(1,128)} %bitcast.7, f32[1,1280]{1,0:T(1,128)} %reshape.28.taps_in, s32[1,64]{1,0:T(1,128)} %bitcast.8, ...), custom_call_target="tpu_custom_call" | custom-call | flops 21474836480 | bytes 4194304 | tf_op jit(solution)/shard_map/pallas_call | solution.py:408
  75.1 2.7 %copy.12 = f32[2,3,32,2048]{3,2,1,0:T(8,128)} copy(f32[2,3,32,2048]{3,2,1,0:T(8,128)} %shard_map.100) | data formatting | bytes 3145728

commit v2 on v1

--- a/solution.py
+++ b/solution.py
@@ -20,6 +20,7 @@
 N_TM = 128
 SIDE = 8
 TAPS_PAD = 1280
+TAPS_ROW = 2048
 MESH = pl.DeviceIdType.MESH
 F32 = jnp.float32
 BF16 = jnp.bfloat16
@@ -158,7 +159,7 @@
     fetch_late = [fetch(9, wiener_in, wiener), fetch(10, tables_in, tables)]
     for copy in fetch_rest:
         copy.wait()
-    band_rows = jnp.broadcast_to(taps[...], (256, TAPS_PAD))
+    band_rows = jnp.broadcast_to(taps[:, 0:TAPS_PAD], (256, TAPS_PAD))
     toep[...] = pltpu.roll(band_rows, 0, 1, stride=1, stride_axis=0).astype(BF16)
     plate_cos, plate_sin = jnp.cos(4.0 * plate[...]), jnp.sin(4.0 * plate[...])
     det_cos, det_sin = jnp.cos(2.0 * det_angle[...]), jnp.sin(2.0 * det_angle[...])
@@ -172,12 +173,6 @@
             trig[1, times, lanes] = sin_t * det_cos[:, lanes] + cos_t * det_sin[:, lanes]
 
     rows[...] = jnp.zeros_like(rows)
-    for copy in first_meta:
-        copy.wait_recv()
-    second_meta = [
-        remote(meta.at[y], meta.at[y], m2_send.at[k], m2_recv.at[k], to)
-        for k, to in enumerate(column)
-    ]
     for copy in halo:
         copy.wait_recv()
 
@@ -232,9 +227,7 @@
 
     lax.fori_loop(0, 8, bin_tiles, 0)
 
-    for copy in second_meta:
-        copy.wait_recv()
-    pending += halo + first_meta + second_meta
+    pending += halo + first_meta
 
     c1, c0 = c, 1 - c
     up = dev(y + c0, z + c1, c)
@@ -242,38 +235,38 @@
     peers = [dev(y + c1 * k, z + c0 * k, c) for k in range(1, SIDE)]
     sibling = dev(y, z, 1 - c)
 
-    def chip(d2, d1):
-        return ((y + 16 - c1 * d1 - c0 * d2) % SIDE) * SIDE + (z + 16 - c0 * d1 - c1 * d2) % SIDE
-
-    def sibling_chip(d2, d1):
-        return ((y + 16 - c0 * d1 - c1 * d2) % SIDE) * SIDE + (z + 16 - c1 * d1 - c0 * d2) % SIDE
-
-    half = pl.ds(pl.multiple_of(c * NTILE, NTILE), NTILE)
-    gathered[y * SIDE + z, half] = local[...].astype(BF16)
-
-    def carry(d2, d1, send, recv, to):
-        piece = gathered.at[chip(d2, d1), half]
+    gathered[c, 0, 0] = local[...].astype(BF16)
+
+    def carry(src, dst, send, recv, to):
         return pltpu.make_async_remote_copy(
-            src_ref=piece, dst_ref=piece, send_sem=send, recv_sem=recv, device_id=to, device_id_type=MESH
+            src_ref=src, dst_ref=dst, send_sem=send, recv_sem=recv, device_id=to, device_id_type=MESH
         )
 
+    def four(d2, h):
+        return gathered.at[c, d2, pl.ds(pl.multiple_of(h * 4, 4), 4)]
+
     def to_peer(k):
-        return carry(0, 0, p1_send.at[k], p1_recv.at[k], peers[k - 1])
-
-    def to_line(d2, d1, step):
-        to = up if step == 1 else down
-        at = ((d2 + step) % SIDE) * SIDE + d1
-        return carry(d2, d1, p2_send.at[at], p2_recv.at[at], to)
-
-    def to_sibling(d2, d1):
-        at = d2 * SIDE + d1
-        return carry(d2, d1, sib_send.at[at], sib_recv.at[at], sibling)
-
-    to_line(0, 0, 1).start()
-    to_line(0, 0, 7).start()
+        src, dst = gathered.at[c, 0, 0], gathered.at[c, 0, k]
+        return carry(src, dst, p1_send.at[k], p1_recv.at[k], peers[k - 1])
+
+    def to_line(d2, h, step):
+        to, then = up if step == 1 else down, (d2 + step) % SIDE
+        at = then * 2 + h
+        return carry(four(d2, h), four(then, h), p2_send.at[at], p2_recv.at[at], to)
+
+    def to_sibling(d2, h):
+        at = d2 * 2 + h
+        return carry(four(d2, h), four(d2, h), sib_send.at[at], sib_recv.at[at], sibling)
+
     for k in (1, 2, 3, 7, 6, 5, 4):
         to_peer(k).start()
-    to_sibling(0, 0).start()
+    for copy in first_meta:
+        copy.wait_recv()
+    second_meta = [
+        remote(meta.at[y], meta.at[y], m2_send.at[k], m2_recv.at[k], to)
+        for k, to in enumerate(column)
+    ]
+    pending += second_meta
 
     row = iota((BPIX, 128), 0)
     lane = iota((BPIX, 128), 1)
@@ -292,63 +285,61 @@
     turn[0:32, :] = high
     turn[32:64, :] = (whole - high.astype(F32)).astype(BF16)
 
-    for d1 in (1, 2, 3, 7, 6, 5, 4):
-        to_peer(d1).wait_recv()
-        to_line(0, d1, 1).start()
-        to_line(0, d1, 7).start()
-        to_sibling(0, d1).start()
-
-    def arrive(d2, d1, step):
-        to_line((d2 + SIDE - step) % SIDE, d1, step).wait_recv()
+    for h in range(2):
+        for d1 in ((1, 2, 3), (7, 6, 5, 4))[h]:
+            to_peer(d1).wait_recv()
+        to_line(0, h, 1).start()
+        to_line(0, h, 7).start()
+        to_sibling(0, h).start()
+    for copy in second_meta:
+        copy.wait_recv()
+
+    def arrive(d2, h, step):
+        to_line((d2 + SIDE - step) % SIDE, h, step).wait_recv()
 
     def members(g):
         k = (g + 1) // 2
         single = (7 - g % 7) // 7
-        for e in range(8):
-            sign, i = e // 4, e % 4
-            d2 = (k + sign * (8 - 2 * k)) % SIDE
-            d1 = (single * sign + (1 - single) * ((g + 1) % 2)) * 4 + i
-            yield d2, d1
+        for sign in range(2):
+            yield (k + sign * (8 - 2 * k)) % SIDE, single * sign + (1 - single) * ((g + 1) % 2)
 
     key_rows = iota((256, 1024), 0).astype(F32).astype(BF16)
     turn_rows = iota((64, 1024), 0) % 32
 
     def each_group(g, state):
-        k = 1 + g // 2
+        k, h = 1 + g // 2, g % 2
 
         @pl.when(g < 6)
         def _():
-            for i in range(4):
-                d1 = (g % 2) * 4 + i
-                for step in (1, 7):
-                    d2 = k if step == 1 else SIDE - k
-                    arrive(d2, d1, step)
-
-                    @pl.when(k < 3)
-                    def _():
-                        to_line(d2, d1, step).start()
-
-                    @pl.when((k == 3) & (g % 2 == (0 if step == 1 else 1)))
-                    def _():
-                        to_line(d2, d1, step).start()
-
-                    to_sibling(d2, d1).start()
+            for step in (1, 7):
+                d2 = k if step == 1 else SIDE - k
+                arrive(d2, h, step)
+
+                @pl.when(k < 3)
+                def _():
+                    to_line(d2, h, step).start()
+
+                @pl.when((k == 3) & (h == (0 if step == 1 else 1)))
+                def _():
+                    to_line(d2, h, step).start()
+
+                to_sibling(d2, h).start()
 
         @pl.when(g == 6)
         def _():
-            for d1 in (0, 4, 1, 5, 2, 6, 3, 7):
-                arrive(4, d1, 1 if d1 < 4 else 7)
-                to_sibling(4, d1).start()
+            for last in range(2):
+                arrive(4, last, 1 if last == 0 else 7)
+                to_sibling(4, last).start()
 
         tiles, codes = [], []
-        for d2, d1 in members(g):
-            to_sibling(d2, d1).wait_recv()
-            mine, other = chip(d2, d1), sibling_chip(d2, d1)
-            first, second = mine * c0 + other * c1, mine * c1 + other * c0
-            tiles += [gathered[first, 0:NTILE], gathered[second, NTILE : 2 * NTILE]]
-            codes.append(
-                meta[first // SIDE, (first % SIDE) * 2] + meta[second // SIDE, (second % SIDE) * 2 + 1]
-            )
+        for d2, quad in members(g):
+            to_sibling(d2, quad).wait_recv()
+            for i in range(4):
+                d1 = quad * 4 + i
+                tiles += [gathered[0, d2, d1], gathered[1, d2, d1]]
+                far, near = (y + SIDE - d2) % SIDE, (z + SIDE - d1) % SIDE
+                across, along = (y + SIDE - d1) % SIDE, (z + SIDE - d2) % SIDE
+                codes.append(meta[far, near * 2] + meta[across, along * 2 + 1])
         tiles, codes = jnp.concatenate(tiles, axis=0), jnp.concatenate(codes, axis=1)
         spectra = dot(tiles, basis[0:384]) + dot(tiles, basis[384:768])
         turn_hot = jnp.where(turn_rows == codes % 32, 1.0, 0.0).astype(BF16)
@@ -378,16 +369,16 @@
         to_peer(k).wait_send()
 
     def sent(n, state):
-        d2, d1 = n // SIDE, n % SIDE
-        to_sibling(d2, d1).wait_send()
+        d2, h = n // 2, n % 2
+        to_sibling(d2, h).wait_send()
 
         @pl.when(d2 > 0)
         def _():
-            to_line((d2 + SIDE - 1) % SIDE, d1, 1).wait_send()
+            to_line((d2 + SIDE - 1) % SIDE, h, 1).wait_send()
 
         return state
 
-    lax.fori_loop(0, 64, sent, 0)
+    lax.fori_loop(0, 16, sent, 0)
 
 
 def column_tables():
@@ -402,7 +393,7 @@
 
 
 def body(timeline, pointing, plate_angle, detector_angle, detector_weight, kernel, tile_owner, tile_block, wiener):
-    taps = jnp.pad(kernel.astype(F32), (0, TAPS_PAD - kernel.shape[0])).reshape(1, TAPS_PAD)
+    taps = jnp.pad(kernel.astype(F32), (0, TAPS_ROW - kernel.shape[0])).reshape(1, TAPS_ROW)
     vmem = pl.BlockSpec(memory_space=pltpu.VMEM)
     dma = pltpu.SemaphoreType.DMA
     return pl.pallas_call(
@@ -417,7 +408,7 @@
             pltpu.VMEM((4, 128), F32),
             pltpu.VMEM((1, DET), F32),
             pltpu.VMEM((1, DET), F32),
-            pltpu.VMEM((1, TAPS_PAD), F32),
+            pltpu.VMEM((1, TAPS_ROW), F32),
             pltpu.VMEM((1, NTILE), jnp.int32),
             pltpu.VMEM((1, NTILE), jnp.int32),
             dma((11,)),
@@ -429,12 +420,12 @@
             pltpu.VMEM((192, PIECE * DGRP), BF16),
             pltpu.VMEM((128, PIECE * DGRP), BF16),
             pltpu.VMEM((NTILE, 384), F32),
-            pltpu.VMEM((64, 2 * NTILE, 384), BF16),
+            pltpu.VMEM((2, SIDE, SIDE, NTILE, 384), BF16),
             pltpu.VMEM((8, 16, 1, 128), jnp.int32),
             pltpu.VMEM((768, 256), BF16),
             pltpu.VMEM((64, 256), BF16),
             dma((2,)), dma((2,)), dma((15,)), dma((15,)), dma((7,)), dma((7,)),
-            dma((8,)), dma((8,)), dma((64,)), dma((64,)), dma((64,)), dma((64,)),
+            dma((8,)), dma((8,)), dma((16,)), dma((16,)), dma((16,)), dma((16,)),
         ],
         compiler_params=pltpu.CompilerParams(
             collective_id=0, has_side_effects=True, vmem_limit_bytes=64 << 20

time: 78.7 us -> 72.5 us (0.921)
  Pallas kernels: 73.8 us -> 68.3 us
    pallas_call x1, Pallas kernels: 73.8 us -> 68.3 us  [body(): pl.pallas_call(map_kernel, out_shape=jax.ShapeDtypeStruct((2, 3, 32, ROWS...]
where the time goes in v2:
time: 72.5 us; the launch traced here: 72.3 us
  Pallas kernels  68.3 us (94%)
  local copies, waits for them, and re-layouts  2.7 us (4%)
  other arithmetic  1.29 us (2%)
    pallas_call x1, Pallas kernels, body(): pl.pallas_call(map_kernel, out_shape=jax.ShapeDtypeStruct((2, 3, 32, ROWS...  68.3 us
    unnamed x1, local copies, waits for them, and re-layouts  2.7 us

profile of v2, /device:TPU:1, one launch (start us, length us, event | category | flops | bytes accessed | tf_op | source)
XLA Modules:
  0.0 72.3 jit_solution(12003547936455026791)
XLA Ops:
  0.0 1.3 %pad_convert_fusion = f32[2048]{0:T(1024)} fusion(bf16[1025]{0:T(1024)(128)(2,1)} %param.15), kind=kLoop, calls=%fused_computation | loop fusion | flops 2048 | bytes 10242 | tf_op jit(solution)/shard_map/reshape | solution.py:396
  1.3 68.3 %shard_map.100 = f32[2,3,32,2048]{3,2,1,0:T(8,128)} custom-call(bf16[512,256]{1,0:T(8,128)(2,1)} %timeline_in.1, s32[512,256]{1,0:T(8,128)} %pointing_in.1, f32[4,128]{1,0:T(4,128)} %bitcast.7, f32[1,256]{1,0:T(1,128)} %bitcast.8, f32[1,256]{1,0:T(1,128)} %bitcast.9, f32[1,2048]{1,0:T(1,128)} %bitcast.6, s32[1,64]{1,0:T(1,128)} %bitcast.10, ...), custom_call_target="tpu_custom_call" | custom-call | flops 21474836480 | bytes 4194304 | tf_op jit(solution)/shard_map/pallas_call | solution.py:399
  69.6 2.7 %copy.12 = f32[2,3,32,2048]{3,2,1,0:T(8,128)} copy(f32[2,3,32,2048]{3,2,1,0:T(8,128)} %shard_map.100) | data formatting | bytes 3145728

commit v3 on v2

--- a/solution.py
+++ b/solution.py
@@ -56,7 +56,7 @@
     return [add(even[k], odd[k]) for k in range(4)] + [sub(even[k], odd[k]) for k in range(4)]
 
 
-def finish_columns(rows, tables, wiener, out):
+def finish_columns(rows, tables, out):
     lines = []
     for r in range(8):
         at = slice(r * 256, r * 256 + 256)
@@ -74,15 +74,14 @@
     for k, (real, imag) in enumerate(eighth(lines)):
         at = slice(k * 256, k * 256 + 256)
         for s in range(3):
-            gain = wiener[s, :, at] * scale
-            out[0, s, :, at] = real[s * 32 : s * 32 + 32] * gain
-            out[1, s, :, at] = imag[s * 32 : s * 32 + 32] * gain
+            out[0, s, :, at] = real[s * 32 : s * 32 + 32] * scale
+            out[1, s, :, at] = imag[s * 32 : s * 32 + 32] * scale
 
 
 def map_kernel(
     timeline_in, pointing_in, plate_in, det_angle_in, det_weight_in, taps_in, owner_in, block_in,
-    wiener_in, tables_in, out,
-    rows, wiener, tables,
+    tables_in, out,
+    rows, tables,
     plate, det_angle, det_weight, taps, owner, block, fetched,
     window, toep, trig, vals, pixels, spread, low_hot, local, gathered, meta, basis, turn,
     halo_send, halo_recv, m1_send, m1_recv, m2_send, m2_recv,
@@ -156,7 +155,7 @@
         for k, to in enumerate(plane)
     ]
 
-    fetch_late = [fetch(9, wiener_in, wiener), fetch(10, tables_in, tables)]
+    fetch_late = [fetch(9, tables_in, tables)]
     for copy in fetch_rest:
         copy.wait()
     band_rows = jnp.broadcast_to(taps[:, 0:TAPS_PAD], (256, TAPS_PAD))
@@ -341,7 +340,7 @@
                 across, along = (y + SIDE - d1) % SIDE, (z + SIDE - d2) % SIDE
                 codes.append(meta[far, near * 2] + meta[across, along * 2 + 1])
         tiles, codes = jnp.concatenate(tiles, axis=0), jnp.concatenate(codes, axis=1)
-        spectra = dot(tiles, basis[0:384]) + dot(tiles, basis[384:768])
+        spectra = dot(jnp.concatenate([tiles, tiles], axis=1), basis[...])
         turn_hot = jnp.where(turn_rows == codes % 32, 1.0, 0.0).astype(BF16)
         turned = dot(turn_hot, turn[...], ((0,), (0,)))
         real, imag = spectra[:, 0:128], spectra[:, 128:256]
@@ -361,7 +360,7 @@
 
     for copy in fetch_late:
         copy.wait()
-    finish_columns(rows, tables, wiener, out)
+    finish_columns(rows, tables, out)
 
     for copy in pending:
         copy.wait_send()
@@ -396,14 +395,13 @@
     taps = jnp.pad(kernel.astype(F32), (0, TAPS_ROW - kernel.shape[0])).reshape(1, TAPS_ROW)
     vmem = pl.BlockSpec(memory_space=pltpu.VMEM)
     dma = pltpu.SemaphoreType.DMA
-    return pl.pallas_call(
+    spectrum = pl.pallas_call(
         map_kernel,
         out_shape=jax.ShapeDtypeStruct((2, 3, 32, ROWS), F32),
-        in_specs=[pl.BlockSpec(memory_space=pl.ANY)] * 10,
+        in_specs=[pl.BlockSpec(memory_space=pl.ANY)] * 9,
         out_specs=vmem,
         scratch_shapes=[
             pltpu.VMEM((ROWS, 256), F32),
-            pltpu.VMEM((3, 32, ROWS), F32),
             pltpu.VMEM((2, 8, 2, 256, 256), BF16),
             pltpu.VMEM((4, 128), F32),
             pltpu.VMEM((1, DET), F32),
@@ -411,7 +409,7 @@
             pltpu.VMEM((1, TAPS_ROW), F32),
             pltpu.VMEM((1, NTILE), jnp.int32),
             pltpu.VMEM((1, NTILE), jnp.int32),
-            dma((11,)),
+            dma((10,)),
             pltpu.VMEM((3 * TS, DET), BF16),
             pltpu.VMEM((256, TAPS_PAD), BF16),
             pltpu.VMEM((2, TS, DET), F32),
@@ -440,9 +438,9 @@
         taps,
         tile_owner.reshape(1, NTILE),
         tile_block.reshape(1, NTILE),
-        wiener,
         jnp.asarray(column_tables()),
     )
+    return spectrum * wiener[None]
 
 
 def solution(mesh):

time: 72.5 us -> 67.6 us (0.932)
  Pallas kernels: 68.3 us -> 63.2 us
  other arithmetic: 1.29 us -> 4.22 us
  local copies, waits for them, and re-layouts: 2.7 us -> 0 us
    pallas_call x1, Pallas kernels: 68.3 us -> 63.2 us  [body(): pl.pallas_call(map_kernel, out_shape=jax.ShapeDtypeStruct((2, 3, 32, ROWS...]
    mul x0 -> x1, other arithmetic: none -> 2.94 us  [body(): return spectrum * wiener[None]]
    unnamed x1 -> x0, local copies, waits for them, and re-layouts: 2.7 us -> none
where the time goes in v3:
time: 67.6 us; the launch traced here: 67.4 us
  Pallas kernels  63.2 us (93%)
  other arithmetic  4.22 us (6%)
    pallas_call x1, Pallas kernels, body(): pl.pallas_call(map_kernel, out_shape=jax.ShapeDtypeStruct((2, 3, 32, ROWS...  63.2 us
    mul x1, other arithmetic, body(): return spectrum * wiener[None]  2.94 us

profile of v3, /device:TPU:1, one launch (start us, length us, event | category | flops | bytes accessed | tf_op | source)
XLA Modules:
  0.0 67.4 jit_solution(1659966794292469425)
XLA Ops:
  0.0 1.3 %pad_convert_fusion = f32[2048]{0:T(1024)} fusion(bf16[1025]{0:T(1024)(128)(2,1)} %param.15), kind=kLoop, calls=%fused_computation.1 | loop fusion | flops 2048 | bytes 10242 | tf_op jit(solution)/shard_map/reshape | solution.py:395
  1.3 63.2 %shard_map.100 = f32[2,3,32,2048]{3,2,1,0:T(8,128)} custom-call(bf16[512,256]{1,0:T(8,128)(2,1)} %timeline_in.1, s32[512,256]{1,0:T(8,128)} %pointing_in.1, f32[4,128]{1,0:T(4,128)} %bitcast.7, f32[1,256]{1,0:T(1,128)} %bitcast.8, f32[1,256]{1,0:T(1,128)} %bitcast.9, f32[1,2048]{1,0:T(1,128)} %bitcast.6, s32[1,64]{1,0:T(1,128)} %bitcast.10, ...), custom_call_target="tpu_custom_call" | custom-call | flops 21474836480 | bytes 4194304 | tf_op jit(solution)/shard_map/pallas_call | solution.py:398
  64.5 2.9 %broadcast_multiply_fusion = f32[2,3,32,2048]{3,2,1,0:T(8,128)} fusion(f32[2,3,32,2048]{3,2,1,0:T(8,128)} %shard_map.100, f32[3,32,2048]{2,1,0:T(8,128)} %param.18), kind=kLoop, calls=%fused_computation | loop fusion | flops 393216 | bytes 3932160 | tf_op jit(solution)/shard_map/mul | solution.py:443

commit v4 on v3

--- a/solution.py
+++ b/solution.py
@@ -389,6 +389,10 @@
     high = table.astype(BF16)
     low = (table - high.astype(np.float64)).astype(BF16)
     return np.stack([high, low])
+
+
+def weigh(spectrum, wiener, out):
+    out[...] = spectrum[...] * wiener[...][None]
 
 
 def body(timeline, pointing, plate_angle, detector_angle, detector_weight, kernel, tile_owner, tile_block, wiener):
@@ -440,7 +444,15 @@
         tile_block.reshape(1, NTILE),
         jnp.asarray(column_tables()),
     )
-    return spectrum * wiener[None]
+    both = pl.BlockSpec((2, 1, 32, ROWS), lambda s: (0, s, 0, 0))
+    return pl.pallas_call(
+        weigh,
+        grid=(3,),
+        out_shape=jax.ShapeDtypeStruct((2, 3, 32, ROWS), F32),
+        in_specs=[both, pl.BlockSpec((1, 32, ROWS), lambda s: (s, 0, 0))],
+        out_specs=both,
+        compiler_params=pltpu.CompilerParams(vmem_limit_bytes=64 << 20),
+    )(spectrum, wiener)
 
 
 def solution(mesh):

time: 67.6 us -> 68.3 us (1.010)
  Pallas kernels: 63.2 us -> 66.7 us
  other arithmetic: 4.22 us -> 1.29 us
    pallas_call x0 -> x1, Pallas kernels: none -> 3.57 us  [body(): pl.pallas_call(weigh, grid=(3,), out_shape=jax.ShapeDtypeStruct((2, 3, 32...]
    mul x1 -> x0, other arithmetic: 2.94 us -> none  [body(): return spectrum * wiener[None]]
where the time goes in v4:
time: 68.3 us; the launch traced here: 68 us
  Pallas kernels  66.7 us (98%)
  other arithmetic  1.29 us (2%)
    pallas_call x1, Pallas kernels, body(): pl.pallas_call(map_kernel, out_shape=jax.ShapeDtypeStruct((2, 3, 32, ROWS...  63.2 us
    pallas_call x1, Pallas kernels, body(): pl.pallas_call(weigh, grid=(3,), out_shape=jax.ShapeDtypeStruct((2, 3, 32...  3.57 us

profile of v4, /device:TPU:1, one launch (start us, length us, event | category | flops | bytes accessed | tf_op | source)
XLA Modules:
  0.0 68.0 jit_solution(17146969445111784733)
XLA Ops:
  0.0 1.3 %pad_convert_fusion = f32[2048]{0:T(1024)} fusion(bf16[1025]{0:T(1024)(128)(2,1)} %param.15), kind=kLoop, calls=%fused_computation | loop fusion | flops 2048 | bytes 10242 | tf_op jit(solution)/shard_map/reshape | solution.py:399
  1.3 63.2 %shard_map.100.spectrum = f32[2,3,32,2048]{3,2,1,0:T(8,128)} custom-call(bf16[512,256]{1,0:T(8,128)(2,1)} %timeline_in.1, s32[512,256]{1,0:T(8,128)} %pointing_in.1, f32[4,128]{1,0:T(4,128)} %bitcast.7, f32[1,256]{1,0:T(1,128)} %bitcast.8, f32[1,256]{1,0:T(1,128)} %bitcast.9, f32[1,2048]{1,0:T(1,128)} %bitcast.6, s32[1,64]{1,0:T(1,128)} %bitcast.10, ...), custom_call_target="tpu_custom_call" | custom-call | flops 21474836480 | bytes 4194304 | tf_op jit(solution)/shard_map/pallas_call | solution.py:402
  64.5 3.6 %shard_map.101 = f32[2,3,32,2048]{3,2,1,0:T(8,128)} custom-call(f32[2,3,32,2048]{3,2,1,0:T(8,128)} %shard_map.100.spectrum, f32[3,32,2048]{2,1,0:T(8,128)} %wiener.1), custom_call_target="tpu_custom_call" | custom-call | tf_op jit(solution)/shard_map/pallas_call | solution.py:448
